TPU v7x, 32 devices: a whole 2x2x4 slice. The times are simulated.
32 devices in a mesh: dp: 16 (over z, y, x), tp: 2 (over core).
Axes of the slice: x: 2, y: 2, z: 4, core: 2. Of those that a mesh axis runs over, the one named last changes fastest.
Arguments:
- inputs: bfloat16 [76800, 512], P(('dp', 'tp')), may hold values from -6 to 6
- page_of: int32 [76800], P('dp'), may hold values from 0 to 3071, as said below
- rel_index: int32 [100, 100], replicated, may hold values from 0 to 360, as said below
- w_qkv: bfloat16 [3, 512, 512], P(None, None, 'tp'), may hold values from -0.25 to 0.25
- qv_bias: float32 [2, 512], P(None, 'tp'), may hold values from -1.5 to 1.5
- w_proj: bfloat16 [512, 512], P('tp'), may hold values from -1 to 1
- w_fc1: bfloat16 [512, 2048], P(None, 'tp'), may hold values from -0.25 to 0.25
- fc1_bias: float32 [2048], P('tp'), may hold values from -1.5 to 1.5
- w_fc2: bfloat16 [2048, 512], P('tp'), may hold values from -0.125 to 0.125
- out_biases: float32 [2, 512], replicated, may hold values from -1.5 to 1.5
- norm_gains: float32 [2, 512], replicated, may hold values from 0.1 to 1.9
- norm_biases: float32 [2, 512], replicated, may hold values from -1.5 to 1.5
- bias_table: float32 [361, 16], P(None, 'tp'), may hold values from -3 to 3
- out_grad: bfloat16 [76800, 512], P(('dp', 'tp')), may hold values from -6 to 6
Outputs:
- block_out: bfloat16 [76800, 512], P(('dp', 'tp'))
- grad_in: bfloat16 [76800, 512], P(('dp', 'tp'))
- g_qkv: float32 [3, 512, 512], P(None, None, 'tp')
- g_qv_bias: float32 [2, 512], P(None, 'tp')
- g_proj: float32 [512, 512], P('tp')
- g_fc1: float32 [512, 2048], P(None, 'tp')
- g_fc1_bias: float32 [2048], P('tp')
- g_fc2: float32 [2048, 512], P('tp')
- g_out_biases: float32 [2, 512], replicated
- g_norm_gains: float32 [2, 512], replicated
- g_norm_biases: float32 [2, 512], replicated
- g_table: float32 [361, 16], P(None, 'tp')
Inputs may be any that keep to these rules, and one draw needn't show every extreme that they name: `page_of`: within each window (100 consecutive patches, row-major), the regions are the rectangles cut by one row boundary and one column boundary; no two windows share a region. `rel_index`: entry [i, j] depends only on the offset of position i from position j within a window, each of the 361 offsets with its own table row.
All inputs are finite; a program needn't handle non-finite values.
Results may differ from a plain program's by a relative error of at most 0.015.
Values may be sent and summed in bfloat16 or wider, within the bound.
No kernel may reach another device: no remote copies, remote signals or barrier semaphores. Data moves between devices by JAX's collectives and lax.ppermute only.
A program may use at most 256 MiB of HBM per device.

v0:
```python
import jax
import jax.numpy as jnp
from jax import lax
from jax.sharding import PartitionSpec as P

HEAD = 32


EPS = 1e-05


def layer_norm(values_in, gain_row, shift_row):
    row_mean = jnp.mean(values_in, axis=-1, keepdims=True)
    centered = values_in - row_mean
    variance = jnp.mean(centered * centered, axis=-1, keepdims=True)
    return centered * lax.rsqrt(variance + EPS) * gain_row + shift_row


def exact_gelu(values_in):
    return jax.nn.gelu(values_in, approximate=False)


def table_from(onehot, table_part, window_size):
    heads_count = table_part.shape[1]
    expanded = jnp.dot(onehot, table_part, precision=lax.Precision.HIGHEST)
    return expanded.reshape(window_size, window_size, heads_count).transpose(2, 0, 1)


def project_qkv(rows_in, w_cat, bias_pair, width):
    projected = jnp.dot(rows_in, w_cat, preferred_element_type=jnp.float32)
    query = (projected[:, :width] + bias_pair[0]).astype(jnp.bfloat16)
    keys = projected[:, width : 2 * width].astype(jnp.bfloat16)
    values = (projected[:, 2 * width :] + bias_pair[1]).astype(jnp.bfloat16)
    return (query, keys, values)


def window_scores(query_part, keys_part, pages_part, table_bias, score_scale):
    raw_scores = (
        jnp.einsum("wqhd,wkhd->whqk", query_part, keys_part, preferred_element_type=jnp.float32)
        * score_scale
        + table_bias[None]
    )
    same_page = pages_part[:, :, None] == pages_part[:, None, :]
    return jnp.where(same_page[:, None], raw_scores, -1e30)


def attend_all(query_split, keys_split, values_split, pages, table_bias, score_scale):

    def attend(block_item):
        query_part, keys_part, values_part, pages_part = block_item
        scores = window_scores(query_part, keys_part, pages_part, table_bias, score_scale)
        row_peak = jnp.max(scores, axis=-1, keepdims=True)
        exponent = jnp.exp(scores - row_peak)
        row_total = jnp.sum(exponent, axis=-1, keepdims=True)
        weights_low = (exponent / row_total).astype(jnp.bfloat16)
        result = jnp.einsum(
            "whqk,wkhd->wqhd", weights_low, values_part, preferred_element_type=jnp.float32
        )
        return (result.astype(jnp.bfloat16), row_peak + jnp.log(row_total))

    return lax.map(attend, (query_split, keys_split, values_split, pages))


def attend_back_all(
    query_split, keys_split, values_split, pages, log_totals, grad_split, table_bias, score_scale
):

    def attend_back(table_sum, block_item):
        query_part, keys_part, values_part, pages_part, log_part, grad_part = block_item
        scores = window_scores(query_part, keys_part, pages_part, table_bias, score_scale)
        weights_f = jnp.exp(scores - log_part)
        grad_weights = jnp.einsum(
            "wqhd,wkhd->whqk", grad_part, values_part, preferred_element_type=jnp.float32
        )
        centre = jnp.sum(grad_weights * weights_f, axis=-1, keepdims=True)
        grad_scores = (weights_f * (grad_weights - centre)).astype(jnp.bfloat16)
        grad_query = (
            jnp.einsum(
                "whqk,wkhd->wqhd", grad_scores, keys_part, preferred_element_type=jnp.float32
            )
            * score_scale
        ).astype(jnp.bfloat16)
        grad_keys = (
            jnp.einsum(
                "whqk,wqhd->wkhd", grad_scores, query_part, preferred_element_type=jnp.float32
            )
            * score_scale
        ).astype(jnp.bfloat16)
        grad_values = jnp.einsum(
            "whqk,wqhd->wkhd",
            weights_f.astype(jnp.bfloat16),
            grad_part,
            preferred_element_type=jnp.float32,
        ).astype(jnp.bfloat16)
        table_sum = table_sum + jnp.sum(grad_scores, axis=0, dtype=jnp.float32)
        return (table_sum, (grad_query, grad_keys, grad_values))

    table_start = jnp.zeros(table_bias.shape, jnp.float32)
    return lax.scan(
        attend_back,
        table_start,
        (query_split, keys_split, values_split, pages, log_totals, grad_split),
    )


def per_device(
    inputs,
    page_of,
    rel_index,
    w_qkv,
    qv_bias,
    w_proj,
    w_fc1,
    fc1_bias,
    w_fc2,
    out_biases,
    norm_gains,
    norm_biases,
    bias_table,
    out_grad,
):
    model_width = inputs.shape[1]
    window_size = rel_index.shape[0]
    group_rows = page_of.shape[0]
    score_scale = HEAD ** (-0.5)
    slots = jnp.arange(bias_table.shape[0], dtype=jnp.int32)
    onehot = (rel_index.reshape(-1)[:, None] == slots[None, :]).astype(jnp.float32)
    stream = inputs.astype(jnp.float32)
    grad_out = out_grad.astype(jnp.float32)
    normed = layer_norm(stream, norm_gains[0], norm_biases[0]).astype(jnp.bfloat16)
    local_width = w_qkv.shape[2]
    heads_here = bias_table.shape[1]
    per_block = 8
    blocks = group_rows // (window_size * per_block)
    table_bias = table_from(onehot, bias_table, window_size)
    pages = page_of.reshape(blocks, per_block, window_size)
    group_normed = lax.all_gather(normed, "tp", axis=0, tiled=True)
    w_cat = jnp.concatenate([w_qkv[0], w_qkv[1], w_qkv[2]], axis=1)
    query, keys, values = project_qkv(group_normed, w_cat, qv_bias, local_width)
    split_shape = (blocks, per_block, window_size, heads_here, HEAD)
    query_split = query.reshape(split_shape)
    keys_split = keys.reshape(split_shape)
    values_split = values.reshape(split_shape)
    attended, log_totals = attend_all(
        query_split, keys_split, values_split, pages, table_bias, score_scale
    )
    attended = attended.reshape(group_rows, local_width)
    branch = lax.psum_scatter(
        jnp.dot(attended, w_proj, preferred_element_type=jnp.float32),
        "tp",
        scatter_dimension=0,
        tiled=True,
    )
    mixed = stream + branch + out_biases[0]
    normed2 = layer_norm(mixed, norm_gains[1], norm_biases[1]).astype(jnp.bfloat16)
    group_normed2 = lax.all_gather(normed2, "tp", axis=0, tiled=True)
    hidden = jnp.dot(group_normed2, w_fc1, preferred_element_type=jnp.float32) + fc1_bias
    active = exact_gelu(hidden).astype(jnp.bfloat16)
    block_out = (
        mixed
        + lax.psum_scatter(
            jnp.dot(active, w_fc2, preferred_element_type=jnp.float32).astype(jnp.bfloat16),
            "tp",
            scatter_dimension=0,
            tiled=True,
        ).astype(jnp.float32)
        + out_biases[1]
    ).astype(jnp.bfloat16)
    group_grad = lax.all_gather(out_grad, "tp", axis=0, tiled=True)
    g_fc2 = jnp.einsum("gf,gd->fd", active, group_grad, preferred_element_type=jnp.float32)
    grad_active = jnp.einsum("gd,fd->gf", group_grad, w_fc2, preferred_element_type=jnp.float32)
    grad_hidden = jax.vjp(exact_gelu, hidden)[1](grad_active)[0].astype(jnp.bfloat16)
    g_fc1_bias = jnp.sum(grad_hidden, axis=0, dtype=jnp.float32)
    g_fc1 = jnp.einsum("gd,gf->df", group_normed2, grad_hidden, preferred_element_type=jnp.float32)
    rows_part = grad_hidden
    grad_normed2 = lax.psum_scatter(
        jnp.einsum("gf,df->gd", rows_part, w_fc1, preferred_element_type=jnp.float32).astype(
            jnp.bfloat16
        ),
        "tp",
        scatter_dimension=0,
        tiled=True,
    ).astype(jnp.float32)
    grad_norm2, g_gain2, g_shift2 = jax.vjp(layer_norm, mixed, norm_gains[1], norm_biases[1])[1](
        grad_normed2
    )
    grad_mixed = grad_out + grad_norm2
    grad_mixed_low = grad_mixed.astype(jnp.bfloat16)
    group_mixed = lax.all_gather(grad_mixed_low, "tp", axis=0, tiled=True)
    g_proj = jnp.einsum("gl,gd->ld", attended, group_mixed, preferred_element_type=jnp.float32)
    grad_attended = jnp.einsum(
        "gd,ld->gl", group_mixed, w_proj, preferred_element_type=jnp.float32
    ).astype(jnp.bfloat16)
    table_grad, (grad_query, grad_keys, grad_values) = attend_back_all(
        query_split,
        keys_split,
        values_split,
        pages,
        log_totals,
        grad_attended.reshape(split_shape),
        table_bias,
        score_scale,
    )
    g_table = jnp.einsum(
        "pt,hp->th", onehot, table_grad.reshape(heads_here, -1), precision=lax.Precision.HIGHEST
    )
    grad_query = grad_query.reshape(group_rows, local_width)
    grad_keys = grad_keys.reshape(group_rows, local_width)
    grad_values = grad_values.reshape(group_rows, local_width)
    grad_qkv = jnp.concatenate([grad_query, grad_keys, grad_values], axis=1)
    g_cat = jnp.einsum("gd,gc->dc", group_normed, grad_qkv, preferred_element_type=jnp.float32)
    g_qkv = g_cat.reshape(model_width, 3, local_width).transpose(1, 0, 2)
    g_qv_bias = jnp.stack(
        [
            jnp.sum(grad_query, axis=0, dtype=jnp.float32),
            jnp.sum(grad_values, axis=0, dtype=jnp.float32),
        ]
    )
    rows_part = grad_qkv
    grad_normed = lax.psum_scatter(
        jnp.einsum("gc,dc->gd", rows_part, w_cat, preferred_element_type=jnp.float32).astype(
            jnp.bfloat16
        ),
        "tp",
        scatter_dimension=0,
        tiled=True,
    ).astype(jnp.float32)
    grad_norm1, g_gain1, g_shift1 = jax.vjp(layer_norm, stream, norm_gains[0], norm_biases[0])[1](
        grad_normed
    )
    grad_in = (grad_mixed + grad_norm1).astype(jnp.bfloat16)
    g_out_biases = jnp.stack([jnp.sum(grad_mixed, axis=0), jnp.sum(grad_out, axis=0)])
    summed = lax.psum((g_qkv, g_qv_bias, g_proj, g_fc1, g_fc1_bias, g_fc2, g_table), "dp")
    shared = lax.psum(
        (g_out_biases, jnp.stack([g_gain1, g_gain2]), jnp.stack([g_shift1, g_shift2])), ("dp", "tp")
    )
    return (
        block_out,
        grad_in,
        summed[0],
        summed[1],
        summed[2],
        summed[3],
        summed[4],
        summed[5],
        shared[0],
        shared[1],
        shared[2],
        summed[6],
    )


def solution(mesh):
    placed = (
        P(("dp", "tp"), None),
        P("dp"),
        P(),
        P(None, None, "tp"),
        P(None, "tp"),
        P("tp", None),
        P(None, "tp"),
        P("tp"),
        P("tp", None),
        P(),
        P(),
        P(),
        P(None, "tp"),
        P(("dp", "tp"), None),
    )
    return jax.shard_map(
        per_device,
        mesh=mesh,
        in_specs=placed,
        out_specs=(
            P(("dp", "tp"), None),
            P(("dp", "tp"), None),
            P(None, None, "tp"),
            P(None, "tp"),
            P("tp", None),
            P(None, "tp"),
            P("tp"),
            P("tp", None),
            P(),
            P(),
            P(),
            P(None, "tp"),
        ),
        check_vma=False,
    )
```

profile of v0, /device:TPU:0, one launch (start us, length us, event | category | flops | bytes accessed | tf_op | source)
XLA Modules:
  0.0 833.5 jit_solution(614018340609937902)
XLA Ops:
  9.5 2.7 fusion.68
  16.9 8.3 fusion.54
  33.5 6.5 fusion.76
  41.6 3.2 fusion.73
  44.8 4.4 copy.66
  49.2 8.5 %reshape.170 = bf16[6,8,100,8,32]{2,1,0,4,3:T(8,128)(2,1)} reshape(bf16[4800,256]{0,1:T(8,128)(2,1)} %copy.66) | data formatting | bytes 4915200 | tf_op jit(solution)/shard_map/reshape | solution.py:143
  57.7 4.4 copy.69
  62.1 4.4 copy.67
  66.5 8.5 %reshape.172 = bf16[6,8,100,8,32]{2,1,0,4,3:T(8,128)(2,1)} reshape(bf16[4800,256]{0,1:T(8,128)(2,1)} %copy.67) | data formatting | bytes 4915200 | tf_op jit(solution)/shard_map/reshape | solution.py:141
  75.0 4.4 copy.70
  79.4 4.4 copy.68
  83.7 8.5 %reshape.173 = bf16[6,8,100,8,32]{2,1,0,4,3:T(8,128)(2,1)} reshape(bf16[4800,256]{0,1:T(8,128)(2,1)} %copy.68) | data formatting | bytes 4915200 | tf_op jit(solution)/shard_map/reshape | solution.py:142
  92.3 4.3 copy.71
  98.6 47.5 %while.29 = (s32[]{:T(128)}, bf16[6,8,100,8,32]{2,1,0,4,3:T(8,128)(2,1)}, f32[6,8,8,100,1]{3,2,1,4,0:T(8,128)}, bf16[6,8,100,8,32]{2,4,3,1,0:T(8,128)(2,1)}, s32...) while((s32[]{:T(128)}, ...), condition=%wide.region_5.6_spmd, body=%wide.region_2.5_spmd.sunk | while | flops 91798400 | bytes 13486589 | solution.py:61
  146.2 6.3 reshape.175
  152.5 6.9 fusion.91
  160.7 19.2 %reduce-scatter.5.cloned.1.call-done = f32[2400,512]{1,0:T(8,128)} async-done(((f32[4800,512]{1,0:T(8,128)}), f32[2400,512]{1,0:T(8,128)}) %reduce-scatter.5.cloned.1.call-update) | async-done | bytes 4915216 | tf_op jit(solution)/shard_map/reduce_scatter | solution.py:148
  179.9 3.1 fusion.85
  189.0 15.5 %all-gather.7.cloned.1.call-done = bf16[4800,512]{1,0:T(8,128)(2,1)} async-done(((bf16[2400,512]{1,0:T(8,128)(2,1)}), bf16[4800,512]{1,0:T(8,128)(2,1)}) %all-gather.7.cloned.1.call-update) | async-done | bytes 4915216 | tf_op jit(solution)/shard_map/all_gather | solution.py:156
  204.5 13.3 %fusion.92 = f32[4800,1024]{1,0:T(8,128)} fusion(bf16[4800,512]{1,0:T(8,128)(2,1)} %all-gather.7.cloned.1.call-done, bf16[512,1024]{1,0:T(8,128)(2,1)S(1)} %copy-done.50), kind=kOutput, calls=%fused_computation.162 | convolution fusion | flops 5033164800 | bytes 25624576 | tf_op jit(solution)/shard_map/dot_general | solution.py:157
  217.8 4.1 all-gather.9.cloned.1.call-done
  221.9 53.8 %convert_reduce_fusion.1 = (f32[1024]{0:T(1024)}, bf16[4800,1024]{1,0:T(8,128)(2,1)S(1)}, f32[4800,1024]{1,0:T(8,128)}) fusion(f32[4800,1024]{1,0:T(8,128)} %fusion.92, f32[1024]{0:T(1024)S(1)} %copy-done.45, bf16[4800,512]{1,0:T(8,128)(2,1)} %all-gather.9.cloned.1.call-done, bf16[1024,512]{1,0:T(8,128)(2,1)S(1)} %copy-done), kind=kOutput, calls=%fused_computation.63 | convolution fusion | flops 5401803776 | bytes 55123968 | tf_op jit(solution)/shard_map/gd,fd->gf/dot_general | solution.py:171
  275.7 3.7 copy-done.52
  279.4 7.2 convolution_convert_fusion.1
  286.7 16.0 %multiply_convert_fusion.1 = bf16[4800,1024]{1,0:T(8,128)(2,1)S(1)} fusion(f32[4800,1024]{1,0:T(8,128)} %get-tuple-element.312, f32[4800,1024]{1,0:T(8,128)} %fusion.92, f32[1024]{0:T(1024)S(1)} %copy-done.45), kind=kLoop, calls=%fused_computation.65 | loop fusion | flops 19660800 | bytes 49156096 | tf_op jit(solution)/shard_map/convert_element_type | solution.py:158
  302.7 3.7 copy-done.13
  306.5 6.9 convolution_convert_fusion.2
  314.1 5.7 fusion.71
  319.8 7.8 reduce-scatter.7.cloned.1.call-done
  327.6 6.6 fusion.84
  334.1 3.5 fusion.81
  337.7 10.8 %fusion.95 = f32[1024,512]{1,0:T(8,128)} fusion(bf16[4800,1024]{1,0:T(8,128)(2,1)} %copy-done.13, bf16[4800,512]{1,0:T(8,128)(2,1)} %all-gather.9.cloned.1.call-done), kind=kOutput, calls=%fused_computation.165 | convolution fusion | flops 5033164800 | bytes 16842752 | tf_op jit(solution)/shard_map/gf,gd->fd/dot_general | solution.py:170
  348.5 11.3 %fusion.94 = f32[512,1024]{1,0:T(8,128)} fusion(bf16[4800,512]{1,0:T(8,128)(2,1)} %all-gather.7.cloned.1.call-done, bf16[4800,1024]{1,0:T(8,128)(2,1)} %copy-done.52), kind=kOutput, calls=%fused_computation.164 | convolution fusion | flops 5033164800 | bytes 16842752 | tf_op jit(solution)/shard_map/gd,gf->df/dot_general | solution.py:174
  359.9 5.3 convolution_convert_fusion.3
  365.2 4.4 copy.74
  369.6 8.6 %reshape.176 = bf16[6,8,100,8,32]{2,1,0,4,3:T(8,128)(2,1)} reshape(bf16[4800,256]{0,1:T(8,128)(2,1)} %copy.74) | data formatting | bytes 4915200 | tf_op jit(solution)/shard_map/reshape | solution.py:200
  380.2 107.7 %while.30 = (s32[]{:T(128)}, f32[8,100,100]{1,2,0:T(8,128)S(1)}, bf16[6,8,100,8,32]{2,4,3,1,0:T(8,128)(2,1)}, bf16[6,8,100,8,32]{2,1,0,4,3:T(8,128)(2,1)}, bf16[...) while((s32[]{:T(128)}, f32[8,100,100]{1,2,0:T(8,128)S(1)}, ...), condition=%wide.region_16.17_spmd.clone, body=%wide.region_13.16_spmd.clone.sunk | while | flops 213657600 | bytes 38841652 | solution.py:99
  391.8 2.5 fusion.148
  394.4 3.8 fusion.150
  412.3 3.8 fusion.150
  430.2 3.8 fusion.150
  448.2 3.8 fusion.150
  463.5 2.5 fusion.148
  466.1 3.8 fusion.150
  484.1 3.8 fusion.150
  488.0 5.7 copy.80
  493.7 6.3 reshape.177
  500.0 3.3 constant_dynamic-update-slice_fusion.2
  503.3 5.3 reshape.178
  508.6 5.6 copy.82
  514.2 6.3 reshape.179
  524.7 4.8 fusion.93
  529.5 7.5 fusion.96
  538.1 9.1 %convolution_convert_fusion = bf16[4800,512]{1,0:T(8,128)(2,1)} fusion(bf16[4800,768]{0,1:T(8,128)(2,1)} %constant_dynamic-update-slice_fusion, bf16[512,256]{1,0:T(8,128)(2,1)S(1)} %copy-done.25, bf16[512,256]{1,0:T(8,128)(2,1)S(1)} %copy-done.26, bf16[512,256]{1,0:T(8,128)(2,1)S(1)} %copy-done.24), kind=kOutput, calls=%fused_computation.84 | convolution fusion | flops 3779690496 | bytes 13074432 | tf_op jit(solution)/shard_map/gc,dc->gd/dot_general | solution.py:221
  547.3 4.2 convert_reduce_fusion.5
  555.7 6.7 fusion.53
  562.4 80.1 %all-reduce.1 = (f32[2,256]{1,0:T(2,128)}, f32[1024]{0:T(1024)}, f32[361,8]{0,1:T(8,128)}) all-reduce(f32[2,256]{1,0:T(2,128)S(1)} %pad_maximum_fusion.6, f32[1024]{0:T(1024)S(1)} %copy-done.49, f32[361,8]{0,1:T(8,128)} %fusion.53), channel_id=1, replica_groups=mesh['dp'=16,'tp'=2] {'dp'}, use_global_device_ids=true, to_apply=%region_23.24 | all-reduce | flops 4424 | bytes 35392 | tf_op jit(solution)/shard_map/psum | solution.py:233
  642.5 109.8 %all-reduce.5.cloned.1.call-done = (f32[3,512,256]{1,2,0:T(8,128)}, f32[256,512]{1,0:T(8,128)}, f32[512,1024]{1,0:T(8,128)}, f32[1024,512]{1,0:T(8,128)}) async-done(((f32[3,512,256]{1,2,0:T(8,128)}, f32[256,512]{1,0:T(8,128)}, f32[512,1024]{1,0:T(8,128)}, f32[1024,512]{1,0:T(8,128)}), (f32[3,512,256]{1,2,0:T(8,128)}, f32[256,512]{1,0:T(8,128)}, f32[512,1024]{1,0:T(8,128)}, ...) | async-done | bytes 6291472 | tf_op jit(solution)/shard_map/psum | solution.py:233
  752.3 3.0 copy.85
  755.3 11.2 %reduce-scatter.11.cloned.1.call-done = bf16[2400,512]{1,0:T(8,128)(2,1)} async-done(((bf16[4800,512]{1,0:T(8,128)(2,1)}), bf16[2400,512]{1,0:T(8,128)(2,1)}) %reduce-scatter.11.cloned.1.call-update) | async-done | bytes 2457616 | tf_op jit(solution)/shard_map/reduce_scatter | solution.py:220
  766.5 3.9 convert_reduce_fusion.2
  771.2 2.6 fusion.72
  775.0 40.9 %all-reduce = (f32[2,512]{1,0:T(2,128)}, f32[2,512]{1,0:T(2,128)}, f32[2,512]{1,0:T(2,128)}) all-reduce(f32[2,512]{1,0:T(2,128)S(1)} %get-tuple-element.338, f32[2,512]{1,0:T(2,128)} %get-tuple-element.339, f32[2,512]{1,0:T(2,128)S(1)} %pad_maximum_fusion.5), channel_id=1, replica_groups=mesh['dp'=16,'tp'=2] {'dp','tp'}, use_global_device_ids=true, to_apply=%region_31.32 | all-reduce | flops 3072 | bytes 24576 | tf_op jit(solution)/shard_map/psum | solution.py:234
  816.0 7.3 add_convert_fusion.1
  (291 shorter events, 170.4 us)
Async XLA Ops:
  7.2 214.7 %copy-start = (bf16[1024,512]{1,0:T(8,128)(2,1)S(1)}, bf16[1024,512]{1,0:T(8,128)(2,1)}, u32[]{:S(2)}) copy-start(bf16[1024,512]{1,0:T(8,128)(2,1)} %param.26) | copy-start | bytes 3145732
  7.2 6.3 copy-start.3
  7.2 5.6 copy-start.46
  7.2 5.7 copy-start.47
  7.2 26.3 %all-gather.5.cloned.1.call-start = ((), (), s32[]{:S(2)}) async-start(), calls=%async_computation.4 | async-start | bytes 7372800 | tf_op jit(solution)/shard_map/all_gather | solution.py:137
  9.5 3.4 copy-start.19
  12.9 172.4 %copy-start.39 = (f32[1,512]{1,0:T(1,128)}, f32[1,512]{1,0:T(1,128)S(1)}, u32[]{:S(2)}) copy-start(f32[1,512]{1,0:T(1,128)S(1)} %get-tuple-element.330) | copy-start | bytes 6148
  15.9 164.0 %reduce-scatter.5.cloned.1.call-start = ((), (), s32[]{:S(2)}) async-start(), calls=%async_computation.5 | async-start | bytes 14745600 | tf_op jit(solution)/shard_map/reduce_scatter | solution.py:148
  16.9 10.3 %copy-start.38 = (s32[10000]{0:T(1024)}, s32[10000]{0:T(1024)S(1)}, u32[]{:S(2)}) copy-start(s32[10000]{0:T(1024)S(1)} %eq.53) | copy-start | bytes 120004
  99.1 2.7 copy-start.5
  107.0 2.6 copy-start.5
  114.8 2.6 copy-start.5
  122.7 2.6 copy-start.5
  130.6 2.6 copy-start.5
  138.4 2.6 copy-start.5
  146.2 13.2 %copy-start.31 = (s32[6,8,100]{2,1,0:T(8,128)}, s32[6,8,100]{2,1,0:T(8,128)S(1)}, u32[]{:S(2)}) copy-start(s32[6,8,100]{2,1,0:T(8,128)S(1)} %get-tuple-element.605) | copy-start | bytes 57604
  159.4 45.0 %all-gather.7.cloned.1.call-start = ((), (), s32[]{:S(2)}) async-start(), calls=%async_computation.6 | async-start | bytes 7372800 | tf_op jit(solution)/shard_map/all_gather | solution.py:156
  183.1 2.2 copy-start.2
  183.1 2.2 copy-start.21
  184.1 1.2 copy-start.33
  185.9 18.6 %copy-start.50 = (bf16[512,1024]{1,0:T(8,128)(2,1)S(1)}, bf16[512,1024]{1,0:T(8,128)(2,1)}, u32[]{:S(2)}) copy-start(bf16[512,1024]{1,0:T(8,128)(2,1)} %param.24) | copy-start | bytes 3145732
  188.3 33.5 %all-gather.9.cloned.1.call-start = ((), (), s32[]{:S(2)}) async-start(), calls=%async_computation.8 | async-start | bytes 7372800 | tf_op jit(solution)/shard_map/all_gather | solution.py:169
  188.9 33.0 %copy-start.45 = (f32[1024]{0:T(1024)S(1)}, f32[1024]{0:T(1024)}, u32[]{:S(2)}) copy-start(f32[1024]{0:T(1024)} %param.25) | copy-start | bytes 12292
  188.9 124.6 %reduce-scatter.9.cloned.1.call-start = ((), (), s32[]{:S(2)}) async-start(), calls=%async_computation.9 | async-start | bytes 7372800 | tf_op jit(solution)/shard_map/reduce_scatter | solution.py:176
  221.9 57.5 %copy-start.51 = (bf16[512,1024]{1,0:T(8,128)(2,1)S(1)}, bf16[512,1024]{1,0:T(8,128)(2,1)}, u32[]{:S(2)}) copy-start(bf16[512,1024]{1,0:T(8,128)(2,1)} %param.24) | copy-start | bytes 3145732
  275.7 3.7 copy-start.52
  286.6 41.0 %reduce-scatter.7.cloned.1.call-start = ((), (), s32[]{:S(2)}) async-start(), calls=%async_computation.7 | async-start | bytes 7372800 | tf_op jit(solution)/shard_map/reduce_scatter | solution.py:161
  302.7 3.8 copy-start.13
  313.4 6.4 copy-start.34
  313.4 46.4 %all-gather.11.cloned.1.call-start = ((), (), s32[]{:S(2)}) async-start(), calls=%async_computation.10 | async-start | bytes 7372800 | tf_op jit(solution)/shard_map/all_gather | solution.py:189
  314.1 13.5 %copy-start.14 = (bf16[2400,512]{1,0:T(8,128)(2,1)S(1)}, bf16[2400,512]{1,0:T(8,128)(2,1)}, u32[]{:S(2)}) copy-start(bf16[2400,512]{1,0:T(8,128)(2,1)} %reduce-scatter.9.cloned.1.call-done) | copy-start | bytes 7372804
  327.6 6.6 copy-start.8
  334.1 3.5 copy-start.7
  337.7 414.6 %all-reduce.5.cloned.1.call-start = ((), (), s32[]{:S(2)}) async-start(), calls=%async_computation.12 | async-start | bytes 12582912 | tf_op jit(solution)/shard_map/psum | solution.py:233
  348.5 11.3 %copy-start.23 = (bf16[256,512]{1,0:T(8,128)(2,1)S(1)}, bf16[256,512]{1,0:T(8,128)(2,1)}, u32[]{:S(2)}) copy-start(bf16[256,512]{1,0:T(8,128)(2,1)} %param.23) | copy-start | bytes 786436
  369.6 10.7 %copy-start.6 = (f32[8,100,100]{1,2,0:T(8,128)S(1)}, f32[8,100,100]{1,2,0:T(8,128)}, u32[]{:S(2)}) copy-start(f32[8,100,100]{1,2,0:T(8,128)} %get-tuple-element.571) | copy-start | bytes 960004
  384.2 4.3 copy-start.1
  402.2 4.3 copy-start.1
  420.0 4.3 copy-start.1
  438.0 4.3 copy-start.1
  455.9 4.3 copy-start.1
  473.9 4.3 copy-start.1
  488.0 12.0 %copy-start.10 = (f32[8,100,100]{1,2,0:T(8,128)}, f32[8,100,100]{1,2,0:T(8,128)S(1)}, u32[]{:S(2)}) copy-start(f32[8,100,100]{1,2,0:T(8,128)S(1)} %get-tuple-element.125) | copy-start | bytes 960004
  520.5 2.6 copy-start.12
  520.5 4.2 copy-start.11
  524.7 4.8 copy-start.17
  537.0 0.9 copy-start.24
  537.0 1.0 copy-start.25
  537.0 1.1 copy-start.26
  537.1 229.4 %reduce-scatter.11.cloned.1.call-start = ((), (), s32[]{:S(2)}) async-start(), calls=%async_computation.11 | async-start | bytes 7372800 | tf_op jit(solution)/shard_map/reduce_scatter | solution.py:220
  547.3 15.1 %copy-start.49 = (f32[1024]{0:T(1024)S(1)}, f32[1024]{0:T(1024)}, u32[]{:S(2)}) copy-start(f32[1024]{0:T(1024)} %get-tuple-element.310) | copy-start | bytes 12292
  551.5 215.0 %copy-start.4 = (bf16[2400,512]{1,0:T(8,128)(2,1)S(1)}, bf16[2400,512]{1,0:T(8,128)(2,1)}, u32[]{:S(2)}) copy-start(bf16[2400,512]{1,0:T(8,128)(2,1)} %param.18) | copy-start | bytes 7372804
  551.5 215.0 %copy-start.20 = (f32[2400]{0:T(1024)S(1)}, f32[2400]{0:T(1024)}, u32[]{:S(2)}) copy-start(f32[2400]{0:T(1024)} %copy-done.19) | copy-start | bytes 28804
  551.5 215.0 %copy-start.37 = (f32[1,512]{1,0:T(1,128)S(1)}, f32[1,512]{1,0:T(1,128)}, u32[]{:S(2)}) copy-start(f32[1,512]{1,0:T(1,128)} %copy-done.36) | copy-start | bytes 6148
  562.4 208.8 %copy-start.28 = (f32[2400]{0:T(1024)S(1)}, f32[2400]{0:T(1024)}, u32[]{:S(2)}) copy-start(f32[2400]{0:T(1024)} %copy-done.27) | copy-start | bytes 28804
  755.3 19.1 %copy-start.41 = (f32[512]{0:T(512)S(1)}, f32[512]{0:T(512)}, u32[]{:S(2)}) copy-start(f32[512]{0:T(512)} %get-tuple-element.255) | copy-start | bytes 6148
  766.5 4.6 copy-start.9
  766.5 7.9 copy-start.42
  766.5 7.9 copy-start.43
  766.5 7.9 copy-start.44
  771.1 2.6 copy-start.35
  816.0 7.3 copy-start.18
  816.0 8.1 copy-start.16
  823.3 2.1 copy-start.15
  (8 other events, 5.2 us)
Sparse Core Ops, SparseCore 0:
  16.0 17.4 all-gather.4
  159.6 20.3 reduce-scatter.4
  188.5 15.9 all-gather.6
  205.9 15.8 all-gather.8
  286.7 13.9 reduce-scatter.8
  313.5 13.9 reduce-scatter.6
  337.8 15.9 all-gather.10
  537.2 215.0 all-reduce.4
  754.7 11.7 reduce-scatter.10
where the time goes:
time: 844 us; the launch traced here: 834 us
  matrix products  263 us (31%)
  local copies, waits for them, and re-layouts  178 us (21%)
  waiting for transfers between devices  169 us (20%)
  blocking collectives  121 us (14%)
  other arithmetic  86.4 us (10%)
  between operations  14.6 us (2%)
    psum x1, waiting for transfers between devices, per_device(): lax.psum((g_qkv, g_qv_bias, g_proj, g_fc1, g_fc1_bias, g_fc2, g_table), '...  110 us
    psum x1, blocking collectives, per_device(): lax.psum((g_qkv, g_qv_bias, g_proj, g_fc1, g_fc1_bias, g_fc2, g_table), '...  80.1 us
    dot_general x1, matrix products, per_device(): jnp.einsum('gd,fd->gf', group_grad, w_fc2, preferred_element_type=jnp.flo...  53.8 us
    psum x1, blocking collectives, per_device(): lax.psum((g_out_biases, jnp.stack([g_gain1, g_gain2]), jnp.stack([g_shift...  40.9 us
    dot_general x12, matrix products, window_scores(): jnp.einsum('wqhd,wkhd->whqk', query_part, keys_part, preferred_element_ty...  28.7 us
    unnamed x108, local copies, waits for them, and re-layouts  25.1 us
    dot_general x6, matrix products, attend_back(): jnp.einsum('whqk,wqhd->wkhd', weights_f.astype(jnp.bfloat16), grad_part,...  22.7 us
    reduce_scatter x1, waiting for transfers between devices, per_device(): lax.psum_scatter(jnp.dot(attended, w_proj, preferred_element_type=jnp.flo...  19.2 us
  transfers between devices with their start and end apart: 9, of which 7 were waited for; matrix products, arithmetic and copies ran while one was open for 13% of the time, Pallas kernels for 0%

commit v1 on v0

v1 whole, which is shorter than its diff:
```python
import functools

import jax
import jax.numpy as jnp
from jax import lax
from jax.experimental import pallas as pl
from jax.experimental.pallas import tpu as pltpu
from jax.sharding import PartitionSpec as P

HEAD = 32
EPS = 1e-05
WIN = 100
KEYS = 104
LANES = 128
SLAB = 256
GROUP = 4
ROWS = GROUP * WIN
LOG2E = 1.4426950408889634
NEG = -1e30
BF = jnp.bfloat16
F32 = jnp.float32
NT = (((1,), (1,)), ((), ()))
TN = (((0,), (0,)), ((), ()))


def dot(a, b):
    return jnp.dot(a, b, preferred_element_type=F32)


def dot_nt(a, b):
    return lax.dot_general(a, b, NT, preferred_element_type=F32)


def dot_tn(a, b):
    return lax.dot_general(a, b, TN, preferred_element_type=F32)


def norm_parts(v):
    mean = jnp.mean(v, axis=-1, keepdims=True)
    centered = v - mean
    var = jnp.mean(centered * centered, axis=-1, keepdims=True)
    r = lax.rsqrt(var + EPS)
    return centered * r, r


def fold_rows(v):
    rows, cols = v.shape
    return jnp.sum(v.reshape(rows // 8, 8, cols), axis=0)


def lane_mask(rows, test):
    lane = lax.broadcasted_iota(jnp.int32, (rows, SLAB), 1)
    return jnp.where(test(lane), 1.0, 0.0).astype(BF)


def attn_fwd_body(
    x_ref, page_ref, wa_ref, wb_ref, qva_ref, qvb_ref, bias_ref, pa_ref, pb_ref, ob_ref, gain_ref, shift_ref,
    mixed_ref, att_ref, n_ref, qkv_ref, p_ref,
    scr, att_scr,
):
    scale = (HEAD ** -0.5) * LOG2E

    @pl.when(pl.program_id(0) == 0)
    def _():
        scr[ROWS:, :] = jnp.zeros((scr.shape[0] - ROWS, scr.shape[1]), F32)

    x = x_ref[...].astype(F32)
    n, _ = norm_parts(x)
    n = (n * gain_ref[0:1] + shift_ref[0:1]).astype(BF)
    n_ref[...] = n
    for s, (w_ref, b_ref) in enumerate(((wa_ref, qva_ref), (wb_ref, qvb_ref))):
        lo = s * SLAB
        scr[:ROWS, lo : lo + SLAB] = dot(n, w_ref[0]) + b_ref[0:1]
        scr[:ROWS, 512 + lo : 512 + lo + SLAB] = dot(n, w_ref[1])
        scr[:ROWS, 1024 + lo : 1024 + lo + SLAB] = dot(n, w_ref[2]) + b_ref[1:2]
    for w in range(GROUP):
        qkv_ref[w] = scr[w * WIN : w * WIN + LANES, :].astype(BF)

    even = lane_mask(LANES, lambda c: (c // HEAD) % 2 == 0)
    odd = lane_mask(LANES, lambda c: (c // HEAD) % 2 == 1)
    low = lane_mask(KEYS, lambda c: c % 128 < 64)[:, :128]
    high = lane_mask(KEYS, lambda c: c % 128 >= 64)[:, :128]
    query_lane = lax.broadcasted_iota(jnp.int32, (1, SLAB), 1) % LANES
    valid = jnp.where(query_lane < WIN, 1.0, 0.0)
    first_head = lax.broadcasted_iota(jnp.int32, (2 * HEAD, LANES), 0) < HEAD

    def window(w, carry):
        pages = jnp.broadcast_to(page_ref[w], (LANES, LANES))
        mask = jnp.where(pages == pages.T, 0.0, NEG)[:KEYS]
        mask = jnp.concatenate([mask, mask], axis=1)
        for s in range(2):
            lo = s * SLAB
            q = qkv_ref[w, :, lo : lo + SLAB]
            k = qkv_ref[w, :KEYS, 512 + lo : 512 + lo + SLAB]
            v = qkv_ref[w, :, 1024 + lo : 1024 + lo + SLAB]
            q2 = jnp.concatenate([q * even, q * odd], axis=0)
            v_t = v.T
            outs = []
            for p in range(4):
                g = p // 2
                kp = k[:, 128 * g : 128 * g + 128] * (low if p % 2 == 0 else high)
                st = dot_nt(kp, q2[:, 128 * g : 128 * g + 128])
                st = st * scale + bias_ref[4 * s + p] + mask
                peak = jnp.max(st, axis=0, keepdims=True)
                e = jnp.exp2(st - peak)
                total = jnp.sum(e, axis=0, keepdims=True)
                pt = (e * (valid / total)).astype(BF)
                p_ref[w, 4 * s + p] = pt
                ot = dot(v_t[64 * p : 64 * p + 64, :KEYS], pt)
                outs.append(jnp.where(first_head, ot[:, :LANES], ot[:, LANES:]))
            att_scr[w, :, lo : lo + SLAB] = jnp.concatenate(outs, axis=0).T
        return carry

    lax.fori_loop(0, GROUP, window, 0)
    for w in range(GROUP):
        scr[w * WIN : w * WIN + WIN, :512] = att_scr[w, :WIN, :]
    att = scr[:ROWS, :512].astype(BF)
    att_ref[...] = att
    mixed_ref[...] = x + ob_ref[0:1] + dot(att[:, :SLAB], pa_ref[...]) + dot(att[:, SLAB:], pb_ref[...])


def gelu_parts(h):
    e = jnp.exp2(h * h * (-0.5 * LOG2E))
    t = 1.0 / (1.0 + (0.3275911 * 0.7071067811865476) * jnp.abs(h))
    poly = t * (
        0.5 * 0.254829592
        + t * (0.5 * -0.284496736 + t * (0.5 * 1.421413741 + t * (0.5 * -1.453152027 + t * (0.5 * 1.061405429))))
    )
    tail = poly * e
    phi = jnp.where(h >= 0, 1.0 - tail, tail)
    return phi, e * 0.3989422804014327


def ffn_body(
    mixed_ref, go_ref, att_ref, w1a_ref, w1b_ref, w2a_ref, w2b_ref, b1a_ref, b1b_ref, ob_ref, gain_ref, shift_ref,
    out_ref, gm_ref, gml_ref, g1_ref, g2_ref, gp_ref, gb1_ref, gs_ref,
    acc1, acc2, accp, accb, accs,
):
    step = pl.program_id(0)

    @pl.when(step == 0)
    def _():
        acc1[...] = jnp.zeros_like(acc1)
        acc2[...] = jnp.zeros_like(acc2)
        accp[...] = jnp.zeros_like(accp)
        accb[...] = jnp.zeros_like(accb)
        accs[...] = jnp.zeros_like(accs)

    mixed = mixed_ref[...]
    nh, r = norm_parts(mixed)
    n2 = (nh * gain_ref[1:2] + shift_ref[1:2]).astype(BF)
    go = go_ref[...]
    y = mixed + ob_ref[1:2]
    gn = jnp.zeros_like(mixed)
    for c in range(4):
        w1_ref, w2_ref, b1_ref = (w1a_ref, w2a_ref, b1a_ref) if c < 2 else (w1b_ref, w2b_ref, b1b_ref)
        col = slice(512 * (c % 2), 512 * (c % 2) + 512)
        full = slice(512 * c, 512 * c + 512)
        h = dot(n2, w1_ref[:, col]) + b1_ref[0:1, col]
        ga = dot_nt(go, w2_ref[col, :])
        phi, density = gelu_parts(h)
        act = (h * phi).astype(BF)
        ghf = ga * (phi + h * density)
        gh = ghf.astype(BF)
        y += dot(act, w2_ref[col, :])
        gn += dot_nt(gh, w1_ref[:, col])
        acc2[full, :] += dot_tn(act, go)
        acc1[:, full] += dot_tn(n2, gh)
        accb[:, full] += fold_rows(ghf)
    out_ref[...] = y.astype(BF)
    gof = go.astype(F32)
    e = gn * gain_ref[1:2]
    gm = gof + r * (
        e - jnp.mean(e, axis=-1, keepdims=True) - nh * jnp.mean(e * nh, axis=-1, keepdims=True)
    )
    gm_ref[...] = gm
    gml = gm.astype(BF)
    gml_ref[...] = gml
    accp[...] += dot_tn(att_ref[...], gml)
    accs[0] += fold_rows(gm)
    accs[1] += fold_rows(gof)
    accs[2] += fold_rows(gn * nh)
    accs[3] += fold_rows(gn)

    @pl.when(step == pl.num_programs(0) - 1)
    def _():
        g1_ref[...] = acc1[...].astype(BF)
        g2_ref[...] = acc2[...].astype(BF)
        gp_ref[...] = accp[...].astype(BF)
        gb1_ref[...] = accb[...]
        gs_ref[...] = accs[...]


def attn_bwd_body(
    x_ref, n_ref, gm_ref, gml_ref, qkv_ref, p_ref, wa_ref, wb_ref, pa_ref, pb_ref, gain_ref,
    gin_ref, gqkv_ref, gt_ref, gqv_ref, gs_ref,
    scr, dpad, acc, acct, accb, accs,
):
    step = pl.program_id(0)
    scale = HEAD ** -0.5

    @pl.when(step == 0)
    def _():
        scr[ROWS:, :] = jnp.zeros((scr.shape[0] - ROWS, scr.shape[1]), F32)
        acc[...] = jnp.zeros_like(acc)
        acct[...] = jnp.zeros_like(acct)
        accb[...] = jnp.zeros_like(accb)
        accs[...] = jnp.zeros_like(accs)

    gml = gml_ref[...]
    scr[:ROWS, :SLAB] = dot_nt(gml, pa_ref[...])
    scr[:ROWS, SLAB : 2 * SLAB] = dot_nt(gml, pb_ref[...])
    row = lax.broadcasted_iota(jnp.int32, (LANES, 512), 0)
    for w in range(GROUP):
        dpad[w, :, :512] = jnp.where(row < WIN, scr[w * WIN : w * WIN + LANES, :512], 0.0)

    even = lane_mask(LANES, lambda c: (c // HEAD) % 2 == 0)
    odd = lane_mask(LANES, lambda c: (c // HEAD) % 2 == 1)
    low = lane_mask(KEYS, lambda c: c % 128 < 64)[:, :128]
    high = lane_mask(KEYS, lambda c: c % 128 >= 64)[:, :128]
    first_head = lax.broadcasted_iota(jnp.int32, (2 * HEAD, LANES), 0) < HEAD
    first_pair = lax.broadcasted_iota(jnp.int32, (KEYS, 128), 1) < 64

    def window(w, carry):
        for s in range(2):
            lo = s * SLAB
            q = qkv_ref[w, :, lo : lo + SLAB]
            k = qkv_ref[w, :, 512 + lo : 512 + lo + SLAB]
            v = qkv_ref[w, :KEYS, 1024 + lo : 1024 + lo + SLAB]
            do = dpad[w, :, lo : lo + SLAB].astype(BF)
            q2 = jnp.concatenate([q * even, q * odd], axis=0)
            d2 = jnp.concatenate([do * even, do * odd], axis=0)
            k_t = k.T
            outs, dks, dvs = [], [], []
            for p in range(4):
                g = p // 2
                cols = slice(128 * g, 128 * g + 128)
                vp = v[:, cols] * (low if p % 2 == 0 else high)
                dp = dot_nt(vp, d2[:, cols])
                pt = p_ref[w, 4 * s + p]
                ptf = pt.astype(F32)
                centre = jnp.sum(dp * ptf, axis=0, keepdims=True)
                ds = ptf * (dp - centre)
                acct[4 * s + p] += ds
                ds = ds.astype(BF)
                qt = dot(k_t[64 * p : 64 * p + 64, :KEYS], ds)
                outs.append(jnp.where(first_head, qt[:, :LANES], qt[:, LANES:]))
                dks.append(dot(ds, q2[:, cols]))
                dvs.append(dot(pt, d2[:, cols]))
            dpad[w, :, lo : lo + SLAB] = jnp.concatenate(outs, axis=0).T * scale
            for g in range(2):
                cols = slice(512 + lo + 128 * g, 512 + lo + 128 * g + 128)
                dpad[w, :KEYS, cols] = jnp.where(first_pair, dks[2 * g], dks[2 * g + 1]) * scale
                cols = slice(1024 + lo + 128 * g, 1024 + lo + 128 * g + 128)
                dpad[w, :KEYS, cols] = jnp.where(first_pair, dvs[2 * g], dvs[2 * g + 1])
        return carry

    lax.fori_loop(0, GROUP, window, 0)
    for w in range(GROUP):
        scr[w * WIN : w * WIN + WIN, :] = dpad[w, :WIN, :]
    accb[0] += fold_rows(scr[:ROWS, :512])
    accb[1] += fold_rows(scr[:ROWS, 1024:])
    n = n_ref[...]
    gn = jnp.zeros((ROWS, 512), F32)
    for i in range(3):
        for s, w_ref in enumerate((wa_ref, wb_ref)):
            cols = slice(512 * i + SLAB * s, 512 * i + SLAB * s + SLAB)
            d = scr[:ROWS, cols].astype(BF)
            acc[2 * i + s] += dot_tn(n, d)
            gn += dot_nt(d, w_ref[i])
    nh, r = norm_parts(x_ref[...].astype(F32))
    e = gn * gain_ref[0:1]
    gin = gm_ref[...] + r * (
        e - jnp.mean(e, axis=-1, keepdims=True) - nh * jnp.mean(e * nh, axis=-1, keepdims=True)
    )
    gin_ref[...] = gin.astype(BF)
    accs[0] += fold_rows(gn * nh)
    accs[1] += fold_rows(gn)

    @pl.when(step == pl.num_programs(0) - 1)
    def _():
        for i in range(3):
            for s in range(2):
                gqkv_ref[s, i] = acc[2 * i + s].astype(BF)
        gt_ref[...] = acct[...]
        gqv_ref[...] = accb[...]
        gs_ref[...] = accs[...]


def shaped(shape, dtype):
    return jax.ShapeDtypeStruct(shape, dtype)


def whole(shape):
    return pl.BlockSpec(shape, lambda i: (0,) * len(shape))


def by_rows(*shape):
    return pl.BlockSpec((ROWS,) + shape, lambda i: (i,) + (0,) * len(shape))


def by_windows(*shape):
    return pl.BlockSpec((GROUP,) + shape, lambda i: (i,) + (0,) * len(shape))


PARAMS = pltpu.CompilerParams(vmem_limit_bytes=60 << 20, dimension_semantics=("arbitrary",))


def attn_fwd(x, pages, wa, wb, qva, qvb, bias, pa, pb, ob, gain, shift):
    rows = x.shape[0]
    windows = rows // WIN
    return pl.pallas_call(
        attn_fwd_body,
        name="attn_fwd",
        grid=(rows // ROWS,),
        in_specs=[by_rows(512), by_windows(1, LANES)] + [whole(a.shape) for a in (wa, wb, qva, qvb, bias, pa, pb, ob, gain, shift)],
        out_specs=[by_rows(512), by_rows(512), by_rows(512), by_windows(LANES, 1536), by_windows(8, KEYS, SLAB)],
        out_shape=[
            shaped((rows, 512), F32),
            shaped((rows, 512), BF),
            shaped((rows, 512), BF),
            shaped((windows, LANES, 1536), BF),
            shaped((windows, 8, KEYS, SLAB), BF),
        ],
        scratch_shapes=[pltpu.VMEM((ROWS + 32, 1536), F32), pltpu.VMEM((GROUP, LANES, 512), F32)],
        compiler_params=PARAMS,
    )(x, pages, wa, wb, qva, qvb, bias, pa, pb, ob, gain, shift)


def ffn(mixed, go, att, w1a, w1b, w2a, w2b, b1a, b1b, ob, gain, shift):
    rows = mixed.shape[0]
    small = [w1a, w1b, w2a, w2b, b1a, b1b, ob, gain, shift]
    return pl.pallas_call(
        ffn_body,
        name="feed_forward",
        grid=(rows // ROWS,),
        in_specs=[by_rows(512)] * 3 + [whole(a.shape) for a in small],
        out_specs=[by_rows(512)] * 3
        + [whole((512, 2048)), whole((2048, 512)), whole((512, 512)), whole((8, 2048)), whole((4, 8, 512))],
        out_shape=[
            shaped((rows, 512), BF),
            shaped((rows, 512), F32),
            shaped((rows, 512), BF),
            shaped((512, 2048), BF),
            shaped((2048, 512), BF),
            shaped((512, 512), BF),
            shaped((8, 2048), F32),
            shaped((4, 8, 512), F32),
        ],
        scratch_shapes=[
            pltpu.VMEM((512, 2048), F32),
            pltpu.VMEM((2048, 512), F32),
            pltpu.VMEM((512, 512), F32),
            pltpu.VMEM((8, 2048), F32),
            pltpu.VMEM((4, 8, 512), F32),
        ],
        compiler_params=PARAMS,
    )(mixed, go, att, *small)


def attn_bwd(x, n, gm, gml, qkv, probs, wa, wb, pa, pb, gain):
    rows = x.shape[0]
    return pl.pallas_call(
        attn_bwd_body,
        name="attn_bwd",
        grid=(rows // ROWS,),
        in_specs=[by_rows(512)] * 4
        + [by_windows(LANES, 1536), by_windows(8, KEYS, SLAB)]
        + [whole(a.shape) for a in (wa, wb, pa, pb, gain)],
        out_specs=[
            by_rows(512),
            whole((2, 3, 512, SLAB)),
            whole((8, KEYS, SLAB)),
            whole((2, 8, 512)),
            whole((2, 8, 512)),
        ],
        out_shape=[
            shaped((rows, 512), BF),
            shaped((2, 3, 512, SLAB), BF),
            shaped((8, KEYS, SLAB), F32),
            shaped((2, 8, 512), F32),
            shaped((2, 8, 512), F32),
        ],
        scratch_shapes=[
            pltpu.VMEM((ROWS + 32, 1536), F32),
            pltpu.VMEM((GROUP, LANES, 1536), F32),
            pltpu.VMEM((6, 512, SLAB), F32),
            pltpu.VMEM((8, KEYS, SLAB), F32),
            pltpu.VMEM((2, 8, 512), F32),
            pltpu.VMEM((2, 8, 512), F32),
        ],
        compiler_params=PARAMS,
    )(x, n, gm, gml, qkv, probs, wa, wb, pa, pb, gain)


def expand_table(rel_index, table):
    heads = table.shape[1]
    slots = jnp.arange(table.shape[0], dtype=jnp.int32)
    onehot = (rel_index.T.reshape(-1)[:, None] == slots[None, :]).astype(F32)
    bias = jnp.dot(onehot, table * LOG2E, precision=lax.Precision.HIGHEST)
    bias = bias.reshape(WIN, WIN, heads).transpose(2, 0, 1)
    bias = jnp.pad(bias, ((0, 0), (0, KEYS - WIN), (0, LANES - WIN)))
    return bias.reshape(heads // 2, 2, KEYS, LANES).transpose(0, 2, 1, 3).reshape(heads // 2, KEYS, SLAB)


def table_grad(rel_index, gt):
    pairs = gt.shape[0]
    g = gt.reshape(pairs, KEYS, 2, LANES)[:, :WIN, :, :WIN].transpose(0, 2, 1, 3).reshape(2 * pairs, WIN * WIN)
    slots = jnp.arange(361, dtype=jnp.int32)
    onehot = (rel_index.T.reshape(-1)[:, None] == slots[None, :]).astype(F32)
    return jnp.einsum("pt,hp->th", onehot, g, precision=lax.Precision.HIGHEST)


SWAP = [(0, 1), (1, 0)]


def dp_exchanges(size):
    bit = 1
    while bit < size:
        yield [(i, i ^ bit) for i in range(size)]
        bit *= 2


def all_sum(v, size, over_tp):
    if over_tp:
        v = v + lax.ppermute(v, "tp", SWAP)
    for perm in dp_exchanges(size):
        v = v + lax.ppermute(v, "dp", perm)
    return v


def local_block(x, pages, rel_index, wa, wb, qva, qvb, pa, pb, w1a, w1b, b1a, b1b, w2a, w2b, ob, gain, shift, ta, tb, go):
    bias = expand_table(rel_index, jnp.concatenate([ta, tb], axis=1))
    mixed, att, n, qkv, probs = attn_fwd(x, pages, wa, wb, qva, qvb, bias, pa, pb, ob, gain, shift)
    out, gm, gml, g1, g2, gp, gb1, gs2 = ffn(mixed, go, att, w1a, w1b, w2a, w2b, b1a, b1b, ob, gain, shift)
    gin, gqkv, gt, gqv, gs1 = attn_bwd(x, n, gm, gml, qkv, probs, wa, wb, pa, pb, gain)
    g_table = table_grad(rel_index, gt)
    return out, gin, g1, g2, gp, gqkv, gb1.sum(0), gs2.sum(1), gqv.sum(1), gs1.sum(1), g_table


def per_device(
    dp_size, inputs, page_of, rel_index, w_qkv, qv_bias, w_proj, w_fc1, fc1_bias, w_fc2, out_biases, norm_gains,
    norm_biases, bias_table, out_grad,
):
    me = lax.axis_index("tp")
    windows = inputs.shape[0] // WIN
    swap = lambda v: lax.ppermute(v, "tp", SWAP)
    pages = lax.dynamic_slice_in_dim(page_of.reshape(2 * windows, WIN), me * windows, windows, 0)
    pages = jnp.pad(pages.astype(F32), ((0, 0), (0, LANES - WIN)), constant_values=-1.0)[:, None, :]
    res = local_block(
        inputs, pages, rel_index, w_qkv, swap(w_qkv), qv_bias, swap(qv_bias), w_proj, swap(w_proj),
        w_fc1, swap(w_fc1), fc1_bias[None], swap(fc1_bias)[None], w_fc2, swap(w_fc2), out_biases, norm_gains,
        norm_biases, bias_table, swap(bias_table), out_grad,
    )
    out, gin, g1, g2, gp, gqkv, gb1, gs2, gqv, gs1, g_table = res
    add = lambda mine, other: all_sum(mine + swap(other), dp_size, False).astype(F32)
    g_qkv = add(gqkv[0], gqkv[1])
    g_proj = add(gp[:SLAB], gp[SLAB:])
    g_fc1 = add(g1[:, :1024], g1[:, 1024:])
    g_fc2 = add(g2[:1024], g2[1024:])
    g_fc1_bias = add(gb1[:1024], gb1[1024:])
    g_qv_bias = add(gqv[:, :SLAB], gqv[:, SLAB:])
    g_tab = add(g_table[:, :8], g_table[:, 8:])
    shared = all_sum(jnp.concatenate([gs2, gs1]), dp_size, True)
    g_out_biases = shared[0:2]
    g_gains = jnp.stack([shared[4], shared[2]])
    g_shifts = jnp.stack([shared[5], shared[3]])
    return out, gin, g_qkv, g_qv_bias, g_proj, g_fc1, g_fc1_bias, g_fc2, g_out_biases, g_gains, g_shifts, g_tab


def solution(mesh):
    rows = P(("dp", "tp"), None)
    placed = (
        rows, P("dp"), P(), P(None, None, "tp"), P(None, "tp"), P("tp", None), P(None, "tp"), P("tp"),
        P("tp", None), P(), P(), P(), P(None, "tp"), rows,
    )
    results = (
        rows, rows, P(None, None, "tp"), P(None, "tp"), P("tp", None), P(None, "tp"), P("tp"), P("tp", None),
        P(), P(), P(), P(None, "tp"),
    )
    return jax.shard_map(
        functools.partial(per_device, mesh.shape["dp"]), mesh=mesh, in_specs=placed, out_specs=results, check_vma=False
    )
```

time: 844 us -> 511 us (0.61); the launches traced: 834 us -> 510 us
  matrix products: 263 us -> 14.6 us
  Pallas kernels: 0 us -> 181 us
  local copies, waits for them, and re-layouts: 178 us -> 16.7 us
  blocking collectives: 121 us -> 0 us
  other arithmetic: 86.4 us -> 23.4 us
  waiting for transfers between devices: 169 us -> 228 us
  starting transfers between devices: 0.37 us -> 45.3 us
  between operations: 14.6 us -> 1.1 us
    dot_general x56 -> x2, matrix products: 263 us -> 14.6 us  [the longest x1 8.4 us: expand_table(): bias = jnp.dot(onehot, table * LOG2E, precision=lax.Precision.HIGHEST)]
    ppermute x0 -> x47, waiting for transfers between devices: none -> 228 us  [the longest x32 223 us: all_sum(): v = v + lax.ppermute(v, 'dp', perm)]
    pallas_call x0 -> x3, Pallas kernels: none -> 181 us  [the longest x1 62.6 us: attn_bwd(): pl.pallas_call(attn_bwd_body, name='attn_bwd', grid=(rows // ROWS,), in_s...]
    psum x2 -> x0, blocking collectives: 121 us -> none  [the longest x1 80.1 us: per_device(): lax.psum((g_qkv, g_qv_bias, g_proj, g_fc1, g_fc1_bias, g_fc2, g_table), '...]
    psum x1 -> x0, waiting for transfers between devices: 110 us -> none  [per_device(): lax.psum((g_qkv, g_qv_bias, g_proj, g_fc1, g_fc1_bias, g_fc2, g_table), '...]
    reshape x11 -> x5, local copies, waits for them, and re-layouts: 62.9 us -> 6.02 us  [the longest x2 2.68 us: table_grad(): gt.reshape(pairs, KEYS, 2, LANES)[:, :WIN, :, :WIN].transpose(0, 2, 1, 3)]
    reduce_sum x22 -> x4, other arithmetic: 46.5 us -> 0.1 us  [the longest x1 0.03 us: local_block(): gs2.sum(1)]
    ppermute x0 -> x47, starting transfers between devices: none -> 45.3 us  [the longest x32 41.5 us: all_sum(): v = v + lax.ppermute(v, 'dp', perm)]
  transfers between devices with their start and end apart: 9 -> 47, of which waited for: 7 -> 20; matrix products, arithmetic and copies ran while one was open for 13% -> 9% of each run, Pallas kernels for 0% -> 24%
where the time goes in v1:
time: 511 us; the launch traced here: 510 us
  waiting for transfers between devices  228 us (45%)
  Pallas kernels  181 us (35%)
  starting transfers between devices  45.3 us (9%)
  other arithmetic  23.4 us (5%)
  local copies, waits for them, and re-layouts  16.7 us (3%)
  matrix products  14.6 us (3%)
    ppermute x32, waiting for transfers between devices, all_sum(): v = v + lax.ppermute(v, 'dp', perm)  223 us
    pallas_call x1, Pallas kernels, attn_bwd(): pl.pallas_call(attn_bwd_body, name='attn_bwd', grid=(rows // ROWS,), in_s...  62.6 us
    pallas_call x1, Pallas kernels, attn_fwd(): pl.pallas_call(attn_fwd_body, name='attn_fwd', grid=(rows // ROWS,), in_s...  61.1 us
    pallas_call x1, Pallas kernels, ffn(): pl.pallas_call(ffn_body, name='feed_forward', grid=(rows // ROWS,), in_sp...  57.2 us
    ppermute x32, starting transfers between devices, all_sum(): v = v + lax.ppermute(v, 'dp', perm)  41.5 us
    add x28, other arithmetic, all_sum(): v = v + lax.ppermute(v, 'dp', perm)  15 us
  transfers between devices with their start and end apart: 47, of which 20 were waited for; matrix products, arithmetic and copies ran while one was open for 9% of the time, Pallas kernels for 24%

profile of v1, /device:TPU:0, one launch (start us, length us, event | category | flops | bytes accessed | tf_op | source)
XLA Modules:
  0.0 509.8 jit_solution(4736525381502345722)
XLA Ops:
  3.0 3.3 collective-permute-done.1.qvb_ref
  6.7 0.9 copy.26
  8.4 8.4 %fusion.1 = f32[10000,16]{0,1:T(8,128)} fusion(s32[10000]{0:T(1024)S(1)} %eq.8, f32[361,8]{0,1:T(8,128)S(1)} %collective-permute-done.2, f32[361,8]{0,1:T(8,128)} %param.26), kind=kOutput, calls=%fused_computation.2 | convolution fusion | flops 696741568 | bytes 703104 | tf_op jit(solution)/shard_map/dot_general | solution.py:400
  16.8 1.6 reshape.44
  18.5 1.0 copy.33
  20.4 61.1 %attn_fwd.1 = (f32[2400,512]{1,0:T(8,128)}, bf16[2400,512]{1,0:T(8,128)(2,1)}, bf16[2400,512]{1,0:T(8,128)(2,1)}, bf16[24,128,1536]{2,1,0:T(8,128)(2,1)}, bf16[24,8,104,256]{3,2,1,0:T(8,128)(2,1)}) custom-call(bf16[2400,512]{1,0:T(8,128)(2,1)} %x_ref.3, f32[24,1,128]{2,1,0:T(1,128)} %bitcast.27, bf16[3,512,256]{2,1,0:T(8,128)(2,1)} %wa_ref.3, ...), custom_call_target="tpu_custom_call" | custom-call | tf_op jit(solution)/shard_map/attn_fwd/pallas_call | solution.py:312
  82.5 57.2 %feed_forward.1 = (bf16[2400,512]{1,0:T(8,128)(2,1)}, f32[2400,512]{1,0:T(8,128)}, bf16[2400,512]{1,0:T(8,128)(2,1)}, bf16[512,2048]{1,0:T(8,128)(2,1)}, bf16[20...) custom-call(f32[2400,512]{1,0:T(8,128)} %get-tuple-element.30.mixed_ref, ...), custom_call_target="tpu_custom_call" | custom-call | tf_op jit(solution)/shard_map/feed_forward/pallas_call | solution.py:333
  139.7 2.4 slice.71
  142.5 1.2 slice.67
  143.8 62.6 %attn_bwd.1 = (bf16[2400,512]{1,0:T(8,128)(2,1)}, bf16[2,3,512,256]{3,2,1,0:T(8,128)(2,1)}, f32[8,104,256]{2,1,0:T(8,128)}, f32[2,8,512]{2,1,0:T(8,128)}, f32[2,8,512]{2,1,0:T(8,128)}) custom-call(bf16[2400,512]{1,0:T(8,128)(2,1)} %x_ref.3, bf16[2400,512]{1,0:T(8,128)(2,1)} %get-tuple-element.33.n_ref, f32[2400,512]{1,0:T(8,128)} %get-tuple-element.34.gm_ref, ...), custom_call_target="tpu_custom_call" | custom-call | tf_op jit(solution)/shard_map/attn_bwd/pallas_call | solution.py:363
  206.4 1.3 slice_bitcast_fusion
  208.2 1.4 slice_add_fusion
  209.6 2.8 collective-permute-start.33
  212.7 2.1 collective-permute-start.8
  214.8 21.5 %collective-permute-done.33 = bf16[1024,512]{1,0:T(8,128)(2,1)S(1)} collective-permute-done((bf16[1024,512]{1,0:T(8,128)(2,1)S(1)}, bf16[1024,512]{1,0:T(8,128)(2,1)S(1)}, u32[]{:S(2)}, u32[]{:S(2)}) %collective-permute-start.33) | collective-permute-done | bytes 1048608 | tf_op jit(solution)/shard_map/ppermute | solution.py:428
  236.6 2.1 collective-permute-start.34
  238.8 20.0 %collective-permute-done.23 = bf16[512,1024]{1,0:T(8,128)(2,1)S(1)} collective-permute-done((bf16[512,1024]{1,0:T(8,128)(2,1)S(1)}, bf16[512,1024]{1,0:T(8,128)(2,1)S(1)}, u32[]{:S(2)}, u32[]{:S(2)}) %collective-permute-start.23) | collective-permute-done | bytes 1048608 | tf_op jit(solution)/shard_map/ppermute | solution.py:428
  259.2 2.1 collective-permute-start.24
  261.3 14.0 %collective-permute-done.8 = bf16[3,512,256]{2,1,0:T(8,128)(2,1)S(1)} collective-permute-done((bf16[3,512,256]{2,1,0:T(8,128)(2,1)S(1)}, bf16[3,512,256]{2,1,0:T(8,128)(2,1)S(1)}, u32[]{:S(2)}, u32[]{:S(2)}) %collective-permute-start.8) | collective-permute-done | bytes 786464 | tf_op jit(solution)/shard_map/ppermute | solution.py:428
  275.3 1.1 add.129
  276.4 1.8 collective-permute-start.9
  279.6 1.5 add.155
  281.8 1.6 collective-permute-start.35
  283.4 1.1 slice_add_fusion.2
  284.5 16.3 %collective-permute-done.9 = bf16[3,512,256]{2,1,0:T(8,128)(2,1)} collective-permute-done((bf16[3,512,256]{2,1,0:T(8,128)(2,1)}, bf16[3,512,256]{2,1,0:T(8,128)(2,1)}, u32[]{:S(2)}, u32[]{:S(2)}) %collective-permute-start.9) | collective-permute-done | bytes 786464 | tf_op jit(solution)/shard_map/ppermute | solution.py:428
  300.8 1.4 collective-permute-start.18
  302.2 2.4 add.130
  304.7 1.6 collective-permute-start.10
  306.8 1.6 add.145
  310.4 3.0 collective-permute-done.28
  313.5 1.5 collective-permute-start.14
  315.0 2.1 collective-permute-done.14
  317.1 1.5 collective-permute-start.29
  318.6 2.1 collective-permute-done.29
  321.3 1.6 reshape.47
  323.0 1.1 reshape.48
  324.2 1.4 collective-permute-start.30
  325.5 1.0 add.139
  326.5 20.3 %collective-permute-done.15 = f32[2,256]{1,0:T(2,128)S(1)} collective-permute-done((f32[2,256]{1,0:T(2,128)S(1)}, f32[2,256]{1,0:T(2,128)S(1)}, u32[]{:S(2)}, u32[]{:S(2)}) %collective-permute-start.15) | collective-permute-done | bytes 2080 | tf_op jit(solution)/shard_map/ppermute | solution.py:428
  347.2 6.2 %fusion = f32[361,16]{0,1:T(8,128)S(1)} fusion(f32[16,10000]{1,0:T(8,128)} %reshape.48, s32[10000]{0:T(1024)S(1)} %eq.8), kind=kOutput, calls=%fused_computation.1 | convolution fusion | flops 696729984 | bytes 703104 | tf_op jit(solution)/shard_map/pt,hp->th/dot_general | solution.py:411
  353.6 1.1 collective-permute-done.42
  354.9 2.8 collective-permute-start.16
  357.9 1.6 add.131
  359.5 1.7 collective-permute-start.43
  361.2 1.5 add.156
  362.7 1.6 collective-permute-start.20
  364.4 2.6 collective-permute-start.11
  367.9 3.2 collective-permute-done.38
  371.1 1.5 collective-permute-start.44
  372.6 2.2 collective-permute-done.44
  374.8 1.5 collective-permute-start.39
  376.3 2.2 collective-permute-done.39
  379.0 30.3 %collective-permute-done.45 = f32[361,8]{0,1:T(8,128)S(1)} collective-permute-done((f32[361,8]{0,1:T(8,128)S(1)}, f32[361,8]{0,1:T(8,128)S(1)}, u32[]{:S(2)}, u32[]{:S(2)}) %collective-permute-start.45) | collective-permute-done | bytes 11584 | tf_op jit(solution)/shard_map/ppermute | solution.py:428
  409.3 2.5 collective-permute-start.40
  411.8 34.4 %collective-permute-done.40 = f32[6,512]{1,0:T(8,128)S(1)} collective-permute-done((f32[6,512]{1,0:T(8,128)S(1)}, f32[6,512]{1,0:T(8,128)S(1)}, u32[]{:S(2)}, u32[]{:S(2)}) %collective-permute-start.40) | collective-permute-done | bytes 12320 | tf_op jit(solution)/shard_map/ppermute | solution.py:428
  446.1 4.6 collective-permute-done.46
  452.5 3.1 collective-permute-done.41
  455.8 1.6 add.146
  457.4 2.9 collective-permute-start.26
  461.6 15.7 %collective-permute-done.21 = bf16[256,512]{1,0:T(8,128)(2,1)S(1)} collective-permute-done((bf16[256,512]{1,0:T(8,128)(2,1)S(1)}, bf16[256,512]{1,0:T(8,128)(2,1)S(1)}, u32[]{:S(2)}, u32[]{:S(2)}) %collective-permute-start.21) | collective-permute-done | bytes 262176 | tf_op jit(solution)/shard_map/ppermute | solution.py:428
  478.1 1.2 add_convert_fusion.2
  479.4 1.5 add_convert_fusion
  480.8 27.5 %collective-permute-done.26 = bf16[512,1024]{1,0:T(8,128)(2,1)S(1)} collective-permute-done((bf16[512,1024]{1,0:T(8,128)(2,1)S(1)}, bf16[512,1024]{1,0:T(8,128)(2,1)S(1)}, u32[]{:S(2)}, u32[]{:S(2)}) %collective-permute-start.26) | collective-permute-done | bytes 1048608 | tf_op jit(solution)/shard_map/ppermute | solution.py:428
  508.3 1.5 add_convert_fusion.1
  (132 shorter events, 19.4 us)
Async XLA Ops:
  0.6 80.8 %collective-permute-start.4 = (bf16[512,1024]{1,0:T(8,128)(2,1)}, bf16[512,1024]{1,0:T(8,128)(2,1)S(1)}, u32[]{:S(2)}, u32[]{:S(2)}) collective-permute-start(bf16[512,1024]{1,0:T(8,128)(2,1)} %w1a_ref.1), channel_id=1, source_target_pairs={{0,1},{1,0},{2,3},{3,2},{4,5},{5,4},{6,7},{7,6},{8,9},{9,8},{10,11... | collective-permute-start | bytes 3145736 | tf_op jit(solution)/shard_map/ppermute | solution.py:447
  1.2 80.3 %collective-permute-start.5 = (bf16[1024,512]{1,0:T(8,128)(2,1)}, bf16[1024,512]{1,0:T(8,128)(2,1)}, u32[]{:S(2)}, u32[]{:S(2)}) collective-permute-start(bf16[1024,512]{1,0:T(8,128)(2,1)} %w2a_ref.1), channel_id=1, source_target_pairs={{0,1},{1,0},{2,3},{3,2},{4,5},{5,4},{6,7},{7,6},{8,9},{9,8},{10,11... | collective-permute-start | bytes 3145736 | tf_op jit(solution)/shard_map/ppermute | solution.py:447
  1.2 18.2 %collective-permute-start = (bf16[3,512,256]{2,1,0:T(8,128)(2,1)}, bf16[3,512,256]{2,1,0:T(8,128)(2,1)S(1)}, u32[]{:S(2)}, u32[]{:S(2)}) collective-permute-start(bf16[3,512,256]{2,1,0:T(8,128)(2,1)} %wa_ref.3), channel_id=1, source_target_pairs={{0,1},{1,0},{2,3},{3,2},{4,5},{5,4},{6,7},{7,6},{8,9},{9,8},{10,11... | collective-permute-start | bytes 2359304 | tf_op jit(solution)/shard_map/ppermute | solution.py:447
  1.7 4.6 collective-permute-start.1
  1.8 6.5 %collective-permute-start.2 = (f32[361,8]{0,1:T(8,128)}, f32[361,8]{0,1:T(8,128)S(1)}, u32[]{:S(2)}, u32[]{:S(2)}) collective-permute-start(f32[361,8]{0,1:T(8,128)} %param.26), channel_id=1, source_target_pairs={{0,1},{1,0},{2,3},{3,2},{4,5},{5,4},{6,7},{7,6},{8,9},{9,8},{10,11... | collective-permute-start | bytes 34664 | tf_op jit(solution)/shard_map/ppermute | solution.py:447
  6.3 10.6 %copy-start.14 = (f32[2,256]{1,0:T(2,128)}, f32[2,256]{1,0:T(2,128)S(1)}, u32[]{:S(2)}) copy-start(f32[2,256]{1,0:T(2,128)S(1)} %collective-permute-done.1.qvb_ref) | copy-start | bytes 6148
  6.3 13.1 %collective-permute-start.3 = (bf16[256,512]{1,0:T(8,128)(2,1)}, bf16[256,512]{1,0:T(8,128)(2,1)S(1)}, u32[]{:S(2)}, u32[]{:S(2)}) collective-permute-start(bf16[256,512]{1,0:T(8,128)(2,1)} %pa_ref.3), channel_id=1, source_target_pairs={{0,1},{1,0},{2,3},{3,2},{4,5},{5,4},{6,7},{7,6},{8,9},{9,8},{10,11... | collective-permute-start | bytes 786440 | tf_op jit(solution)/shard_map/ppermute | solution.py:447
  8.3 73.2 %collective-permute-start.6 = (f32[1024]{0:T(1024)}, f32[1024]{0:T(1024)S(1)}, u32[]{:S(2)}, u32[]{:S(2)}) collective-permute-start(f32[1024]{0:T(1024)} %param.21), channel_id=1, source_target_pairs={{0,1},{1,0},{2,3},{3,2},{4,5},{5,4},{6,7},{7,6},{8,9},{9,8},{10,11... | collective-permute-start | bytes 12296 | tf_op jit(solution)/shard_map/ppermute | solution.py:447
  19.4 0.7 copy-start.6
  19.4 1.0 copy-start
  81.5 0.6 copy-start.13
  81.5 1.0 copy-start.5
  139.7 2.8 copy-start.1
  142.1 66.1 %collective-permute-start.32 = (bf16[1024,512]{1,0:T(8,128)(2,1)}, bf16[1024,512]{1,0:T(8,128)(2,1)}, u32[]{:S(2)}, u32[]{:S(2)}) collective-permute-start(bf16[1024,512]{1,0:T(8,128)(2,1)} %slice.71), channel_id=1, source_target_pairs={{0,1},{1,0},{2,3},{3,2},{4,5},{5,4},{6,7},{7,6},{8,9},{9,8},{10,11... | collective-permute-start | bytes 3145736 | tf_op jit(solution)/shard_map/ppermute | solution.py:447
  143.6 68.7 %collective-permute-start.22 = (bf16[512,1024]{1,0:T(8,128)(2,1)}, bf16[512,1024]{1,0:T(8,128)(2,1)S(1)}, u32[]{:S(2)}, u32[]{:S(2)}) collective-permute-start(bf16[512,1024]{1,0:T(8,128)(2,1)} %slice.67), channel_id=1, source_target_pairs={{0,1},{1,0},{2,3},{3,2},{4,5},{5,4},{6,7},{7,6},{8,9},{9,8},{10,11... | collective-permute-start | bytes 3145736 | tf_op jit(solution)/shard_map/ppermute | solution.py:447
  143.8 64.4 %copy-start.3 = (bf16[2048,512]{1,0:T(8,128)(2,1)S(1)}, bf16[2048,512]{1,0:T(8,128)(2,1)}, u32[]{:S(2)}) copy-start(bf16[2048,512]{1,0:T(8,128)(2,1)} %get-tuple-element.44) | copy-start | bytes 6291460
  206.4 5.9 %copy-start.2 = (bf16[512,2048]{1,0:T(8,128)(2,1)S(1)}, bf16[512,2048]{1,0:T(8,128)(2,1)}, u32[]{:S(2)}) copy-start(bf16[512,2048]{1,0:T(8,128)(2,1)} %get-tuple-element.42) | copy-start | bytes 6291460
  207.8 4.8 copy-start.4
  207.8 4.8 collective-permute-start.7
  209.6 26.7 %collective-permute-start.33 = (bf16[1024,512]{1,0:T(8,128)(2,1)S(1)}, bf16[1024,512]{1,0:T(8,128)(2,1)S(1)}, u32[]{:S(2)}, u32[]{:S(2)}) collective-permute-start(bf16[1024,512]{1,0:T(8,128)(2,1)S(1)} %slice_add_fusion), channel_id=1, source_target_pairs={{0,2},{2,0},{4,6},{6,4},{8,10},{10,8},{12,14},{14,12},{16,18},{18,... | collective-permute-start | bytes 3145736 | tf_op jit(solution)/shard_map/ppermute | solution.py:428
  212.5 46.2 %collective-permute-start.23 = (bf16[512,1024]{1,0:T(8,128)(2,1)S(1)}, bf16[512,1024]{1,0:T(8,128)(2,1)S(1)}, u32[]{:S(2)}, u32[]{:S(2)}) collective-permute-start(bf16[512,1024]{1,0:T(8,128)(2,1)S(1)} %slice_add_fusion.1), channel_id=1, source_target_pairs={{0,2},{2,0},{4,6},{6,4},{8,10},{10,8},{12,14},{14,12},{16,18},{18,... | collective-permute-start | bytes 3145736 | tf_op jit(solution)/shard_map/ppermute | solution.py:428
  212.7 62.6 %collective-permute-start.8 = (bf16[3,512,256]{2,1,0:T(8,128)(2,1)S(1)}, bf16[3,512,256]{2,1,0:T(8,128)(2,1)S(1)}, u32[]{:S(2)}, u32[]{:S(2)}) collective-permute-start(bf16[3,512,256]{2,1,0:T(8,128)(2,1)S(1)} %bitcast_add_fusion), channel_id=1, source_target_pairs={{0,2},{2,0},{4,6},{6,4},{8,10},{10,8},{12,14},{14,12},{16,18},{18,... | collective-permute-start | bytes 2359304 | tf_op jit(solution)/shard_map/ppermute | solution.py:428
  236.6 41.5 %copy-start.7 = (bf16[512,512]{1,0:T(8,128)(2,1)S(1)}, bf16[512,512]{1,0:T(8,128)(2,1)}, u32[]{:S(2)}) copy-start(bf16[512,512]{1,0:T(8,128)(2,1)} %get-tuple-element.41) | copy-start | bytes 1572868
  236.6 42.2 %copy-start.12 = (f32[2,8,512]{2,1,0:T(8,128)S(1)}, f32[2,8,512]{2,1,0:T(8,128)}, u32[]{:S(2)}) copy-start(f32[2,8,512]{2,1,0:T(8,128)} %get-tuple-element.40) | copy-start | bytes 98308
  236.6 42.3 %copy-start.10 = (f32[8,2048]{1,0:T(8,128)S(1)}, f32[8,2048]{1,0:T(8,128)}, u32[]{:S(2)}) copy-start(f32[8,2048]{1,0:T(8,128)} %get-tuple-element.43) | copy-start | bytes 196612
  236.6 42.9 %collective-permute-start.34 = (bf16[1024,512]{1,0:T(8,128)(2,1)S(1)}, bf16[1024,512]{1,0:T(8,128)(2,1)}, u32[]{:S(2)}, u32[]{:S(2)}) collective-permute-start(bf16[1024,512]{1,0:T(8,128)(2,1)S(1)} %add.154), channel_id=1, source_target_pairs={{0,4},{2,6},{4,0},{6,2},{8,12},{10,14},{12,8},{14,10},{16,20},{18,... | collective-permute-start | bytes 3145736 | tf_op jit(solution)/shard_map/ppermute | solution.py:428
  259.2 47.1 %collective-permute-start.24 = (bf16[512,1024]{1,0:T(8,128)(2,1)S(1)}, bf16[512,1024]{1,0:T(8,128)(2,1)}, u32[]{:S(2)}, u32[]{:S(2)}) collective-permute-start(bf16[512,1024]{1,0:T(8,128)(2,1)S(1)} %add.144), channel_id=1, source_target_pairs={{0,4},{2,6},{4,0},{6,2},{8,12},{10,14},{12,8},{14,10},{16,20},{18,... | collective-permute-start | bytes 3145736 | tf_op jit(solution)/shard_map/ppermute | solution.py:428
  276.4 24.4 %collective-permute-start.9 = (bf16[3,512,256]{2,1,0:T(8,128)(2,1)}, bf16[3,512,256]{2,1,0:T(8,128)(2,1)}, u32[]{:S(2)}, u32[]{:S(2)}) collective-permute-start(bf16[3,512,256]{2,1,0:T(8,128)(2,1)} %add.129), channel_id=1, source_target_pairs={{0,4},{2,6},{4,0},{6,2},{8,12},{10,14},{12,8},{14,10},{16,20},{18,... | collective-permute-start | bytes 2359304 | tf_op jit(solution)/shard_map/ppermute | solution.py:428
  278.9 2.3 collective-permute-start.17
  278.9 25.7 %collective-permute-start.12 = (f32[2,256]{1,0:T(2,128)S(1)}, f32[2,256]{1,0:T(2,128)S(1)}, u32[]{:S(2)}, u32[]{:S(2)}) collective-permute-start(f32[2,256]{1,0:T(2,128)S(1)} %slice.81), channel_id=1, source_target_pairs={{0,1},{1,0},{2,3},{3,2},{4,5},{5,4},{6,7},{7,6},{8,9},{9,8},{10,11... | collective-permute-start | bytes 6152 | tf_op jit(solution)/shard_map/ppermute | solution.py:447
  279.5 28.9 %collective-permute-start.27 = (f32[1024]{0:T(1024)S(1)}, f32[1024]{0:T(1024)S(1)}, u32[]{:S(2)}, u32[]{:S(2)}) collective-permute-start(f32[1024]{0:T(1024)S(1)} %slice.83), channel_id=1, source_target_pairs={{0,1},{1,0},{2,3},{3,2},{4,5},{5,4},{6,7},{7,6},{8,9},{9,8},{10,11... | collective-permute-start | bytes 12296 | tf_op jit(solution)/shard_map/ppermute | solution.py:447
  281.1 0.7 copy-start.8
  281.8 77.6 %collective-permute-start.35 = (bf16[1024,512]{1,0:T(8,128)(2,1)S(1)}, bf16[1024,512]{1,0:T(8,128)(2,1)}, u32[]{:S(2)}, u32[]{:S(2)}) collective-permute-start(bf16[1024,512]{1,0:T(8,128)(2,1)S(1)} %add.155), channel_id=1, source_target_pairs={{0,8},{2,10},{4,12},{6,14},{8,0},{10,2},{12,4},{14,6},{16,24},{18,... | collective-permute-start | bytes 3145736 | tf_op jit(solution)/shard_map/ppermute | solution.py:428
  300.8 23.4 %collective-permute-start.18 = (bf16[256,512]{1,0:T(8,128)(2,1)S(1)}, bf16[256,512]{1,0:T(8,128)(2,1)}, u32[]{:S(2)}, u32[]{:S(2)}) collective-permute-start(bf16[256,512]{1,0:T(8,128)(2,1)S(1)} %slice_add_fusion.2), channel_id=1, source_target_pairs={{0,2},{2,0},{4,6},{6,4},{8,10},{10,8},{12,14},{14,12},{16,18},{18,... | collective-permute-start | bytes 786440 | tf_op jit(solution)/shard_map/ppermute | solution.py:428
  304.7 53.0 %collective-permute-start.10 = (bf16[3,512,256]{2,1,0:T(8,128)(2,1)}, bf16[3,512,256]{2,1,0:T(8,128)(2,1)}, u32[]{:S(2)}, u32[]{:S(2)}) collective-permute-start(bf16[3,512,256]{2,1,0:T(8,128)(2,1)} %add.130), channel_id=1, source_target_pairs={{0,8},{2,10},{4,12},{6,14},{8,0},{10,2},{12,4},{14,6},{16,24},{18,... | collective-permute-start | bytes 2359304 | tf_op jit(solution)/shard_map/ppermute | solution.py:428
  306.3 3.6 collective-permute-start.13
  308.4 147.4 %collective-permute-start.25 = (bf16[512,1024]{1,0:T(8,128)(2,1)S(1)}, bf16[512,1024]{1,0:T(8,128)(2,1)}, u32[]{:S(2)}, u32[]{:S(2)}) collective-permute-start(bf16[512,1024]{1,0:T(8,128)(2,1)S(1)} %add.145), channel_id=1, source_target_pairs={{0,8},{2,10},{4,12},{6,14},{8,0},{10,2},{12,4},{14,6},{16,24},{18,... | collective-permute-start | bytes 3145736 | tf_op jit(solution)/shard_map/ppermute | solution.py:428
  309.9 3.6 collective-permute-start.28
  313.5 3.6 collective-permute-start.14
  317.1 3.6 collective-permute-start.29
  320.7 26.2 %collective-permute-start.15 = (f32[2,256]{1,0:T(2,128)S(1)}, f32[2,256]{1,0:T(2,128)S(1)}, u32[]{:S(2)}, u32[]{:S(2)}) collective-permute-start(f32[2,256]{1,0:T(2,128)S(1)} %add.135), channel_id=1, source_target_pairs={{0,8},{2,10},{4,12},{6,14},{8,0},{10,2},{12,4},{14,6},{16,24},{18,... | collective-permute-start | bytes 6152 | tf_op jit(solution)/shard_map/ppermute | solution.py:428
  324.2 29.3 %collective-permute-start.30 = (f32[1024]{0:T(1024)S(1)}, f32[1024]{0:T(1024)S(1)}, u32[]{:S(2)}, u32[]{:S(2)}) collective-permute-start(f32[1024]{0:T(1024)S(1)} %add.150), channel_id=1, source_target_pairs={{0,8},{2,10},{4,12},{6,14},{8,0},{10,2},{12,4},{14,6},{16,24},{18,... | collective-permute-start | bytes 12296 | tf_op jit(solution)/shard_map/ppermute | solution.py:428
  326.5 26.9 %copy-start.11 = (f32[2,8,512]{2,1,0:T(8,128)S(1)}, f32[2,8,512]{2,1,0:T(8,128)}, u32[]{:S(2)}) copy-start(f32[2,8,512]{2,1,0:T(8,128)} %get-tuple-element.46) | copy-start | bytes 98308
  326.5 26.9 %copy-start.9 = (f32[4,8,512]{2,1,0:T(8,128)S(1)}, f32[4,8,512]{2,1,0:T(8,128)}, u32[]{:S(2)}) copy-start(f32[4,8,512]{2,1,0:T(8,128)} %get-tuple-element.45) | copy-start | bytes 196612
  346.8 8.1 %collective-permute-start.19 = (bf16[256,512]{1,0:T(8,128)(2,1)S(1)}, bf16[256,512]{1,0:T(8,128)(2,1)S(1)}, u32[]{:S(2)}, u32[]{:S(2)}) collective-permute-start(bf16[256,512]{1,0:T(8,128)(2,1)S(1)} %add.139), channel_id=1, source_target_pairs={{0,4},{2,6},{4,0},{6,2},{8,12},{10,14},{12,8},{14,10},{16,20},{18,... | collective-permute-start | bytes 786440 | tf_op jit(solution)/shard_map/ppermute | solution.py:428
  353.5 1.2 collective-permute-start.42
  354.7 9.6 %collective-permute-start.37 = (f32[6,512]{1,0:T(8,128)S(1)}, f32[6,512]{1,0:T(8,128)S(1)}, u32[]{:S(2)}, u32[]{:S(2)}) collective-permute-start(f32[6,512]{1,0:T(8,128)S(1)} %pad_maximum_fusion), channel_id=1, source_target_pairs={{0,1},{1,0},{2,3},{3,2},{4,5},{5,4},{6,7},{7,6},{8,9},{9,8},{10,11... | collective-permute-start | bytes 36872 | tf_op jit(solution)/shard_map/ppermute | solution.py:426
  354.9 7.8 %collective-permute-start.16 = (f32[2,256]{1,0:T(2,128)S(1)}, f32[2,256]{1,0:T(2,128)S(1)}, u32[]{:S(2)}, u32[]{:S(2)}) collective-permute-start(f32[2,256]{1,0:T(2,128)S(1)} %add.136), channel_id=1, source_target_pairs={{0,16},{2,18},{4,20},{6,22},{8,24},{10,26},{12,28},{14,30},{16,0},... | collective-permute-start | bytes 6152 | tf_op jit(solution)/shard_map/ppermute | solution.py:428
  357.7 9.3 %collective-permute-start.31 = (f32[1024]{0:T(1024)S(1)}, f32[1024]{0:T(1024)S(1)}, u32[]{:S(2)}, u32[]{:S(2)}) collective-permute-start(f32[1024]{0:T(1024)S(1)} %add.151), channel_id=1, source_target_pairs={{0,16},{2,18},{4,20},{6,22},{8,24},{10,26},{12,28},{14,30},{16,0},... | collective-permute-start | bytes 12296 | tf_op jit(solution)/shard_map/ppermute | solution.py:428
  359.5 7.8 %collective-permute-start.43 = (f32[361,8]{0,1:T(8,128)S(1)}, f32[361,8]{0,1:T(8,128)S(1)}, u32[]{:S(2)}, u32[]{:S(2)}) collective-permute-start(f32[361,8]{0,1:T(8,128)S(1)} %slice_add_fusion.3), channel_id=1, source_target_pairs={{0,2},{2,0},{4,6},{6,4},{8,10},{10,8},{12,14},{14,12},{16,18},{18,... | collective-permute-start | bytes 34664 | tf_op jit(solution)/shard_map/ppermute | solution.py:428
  362.7 92.9 %collective-permute-start.20 = (bf16[256,512]{1,0:T(8,128)(2,1)S(1)}, bf16[256,512]{1,0:T(8,128)(2,1)S(1)}, u32[]{:S(2)}, u32[]{:S(2)}) collective-permute-start(bf16[256,512]{1,0:T(8,128)(2,1)S(1)} %add.140), channel_id=1, source_target_pairs={{0,8},{2,10},{4,12},{6,14},{8,0},{10,2},{12,4},{14,6},{16,24},{18,... | collective-permute-start | bytes 786440 | tf_op jit(solution)/shard_map/ppermute | solution.py:428
  364.4 113.7 %collective-permute-start.11 = (bf16[3,512,256]{2,1,0:T(8,128)(2,1)S(1)}, bf16[3,512,256]{2,1,0:T(8,128)(2,1)S(1)}, u32[]{:S(2)}, u32[]{:S(2)}) collective-permute-start(bf16[3,512,256]{2,1,0:T(8,128)(2,1)S(1)} %add.131), channel_id=1, source_target_pairs={{0,16},{2,18},{4,20},{6,22},{8,24},{10,26},{12,28},{14,30},{16,0},... | collective-permute-start | bytes 2359304 | tf_op jit(solution)/shard_map/ppermute | solution.py:428
  367.0 112.4 %collective-permute-start.36 = (bf16[1024,512]{1,0:T(8,128)(2,1)S(1)}, bf16[1024,512]{1,0:T(8,128)(2,1)S(1)}, u32[]{:S(2)}, u32[]{:S(2)}) collective-permute-start(bf16[1024,512]{1,0:T(8,128)(2,1)S(1)} %add.156), channel_id=1, source_target_pairs={{0,16},{2,18},{4,20},{6,22},{8,24},{10,26},{12,28},{14,30},{16,0},... | collective-permute-start | bytes 3145736 | tf_op jit(solution)/shard_map/ppermute | solution.py:428
  367.3 3.8 collective-permute-start.38
  371.1 3.7 collective-permute-start.44
  374.8 3.7 collective-permute-start.39
  378.6 30.7 %collective-permute-start.45 = (f32[361,8]{0,1:T(8,128)S(1)}, f32[361,8]{0,1:T(8,128)S(1)}, u32[]{:S(2)}, u32[]{:S(2)}) collective-permute-start(f32[361,8]{0,1:T(8,128)S(1)} %add.165), channel_id=1, source_target_pairs={{0,8},{2,10},{4,12},{6,14},{8,0},{10,2},{12,4},{14,6},{16,24},{18,... | collective-permute-start | bytes 34664 | tf_op jit(solution)/shard_map/ppermute | solution.py:428
  409.3 36.9 %collective-permute-start.40 = (f32[6,512]{1,0:T(8,128)S(1)}, f32[6,512]{1,0:T(8,128)S(1)}, u32[]{:S(2)}, u32[]{:S(2)}) collective-permute-start(f32[6,512]{1,0:T(8,128)S(1)} %add.160), channel_id=1, source_target_pairs={{0,8},{2,10},{4,12},{6,14},{8,0},{10,2},{12,4},{14,6},{16,24},{18,... | collective-permute-start | bytes 36872 | tf_op jit(solution)/shard_map/ppermute | solution.py:428
  446.1 4.6 collective-permute-start.46
  450.7 4.9 collective-permute-start.41
  455.7 21.6 %collective-permute-start.21 = (bf16[256,512]{1,0:T(8,128)(2,1)S(1)}, bf16[256,512]{1,0:T(8,128)(2,1)S(1)}, u32[]{:S(2)}, u32[]{:S(2)}) collective-permute-start(bf16[256,512]{1,0:T(8,128)(2,1)S(1)} %add.141), channel_id=1, source_target_pairs={{0,16},{2,18},{4,20},{6,22},{8,24},{10,26},{12,28},{14,30},{16,0},... | collective-permute-start | bytes 786440 | tf_op jit(solution)/shard_map/ppermute | solution.py:428
  457.4 50.9 %collective-permute-start.26 = (bf16[512,1024]{1,0:T(8,128)(2,1)S(1)}, bf16[512,1024]{1,0:T(8,128)(2,1)S(1)}, u32[]{:S(2)}, u32[]{:S(2)}) collective-permute-start(bf16[512,1024]{1,0:T(8,128)(2,1)S(1)} %add.146), channel_id=1, source_target_pairs={{0,16},{2,18},{4,20},{6,22},{8,24},{10,26},{12,28},{14,30},{16,0},... | collective-permute-start | bytes 3145736 | tf_op jit(solution)/shard_map/ppermute | solution.py:428
